TPU v7x, 32 devices: a whole 2x2x4 slice. The times are simulated.
32 devices in a mesh: dp: 4 (over x, core), seq: 8 (over z, y).
Axes of the slice: x: 2, y: 2, z: 4, core: 2. Of those that a mesh axis runs over, the one named last changes fastest.
Arguments:
- queries: bfloat16 [4, 2048, 2048], P('dp', 'seq'), may hold values from -8 to 8
- key_states: bfloat16 [4, 2048, 512], P('dp', 'seq'), may hold values from -6 to 6
- value_states: bfloat16 [4, 2048, 512], P('dp', 'seq'), may hold values from -6 to 6
- block_picks: int32 [4, 3, 8], P('dp'), may hold values from 0 to 1
- out_weight: bfloat16 [2048, 2048], P(('dp', 'seq')), may hold values from -0.5 to 0.5
- out_grad: bfloat16 [4, 2048, 2048], P('dp', 'seq'), may hold values from -4 to 4
Outputs:
- layer_out: bfloat16 [4, 2048, 2048], P('dp', 'seq')
- query_grad: bfloat16 [4, 2048, 2048], P('dp', 'seq')
- key_grad: bfloat16 [4, 2048, 512], P('dp', 'seq')
- value_grad: bfloat16 [4, 2048, 512], P('dp', 'seq')
All inputs are finite; a program needn't handle non-finite values.
Results may differ from a plain program's by a relative error of at most 0.025.
Values may be sent and summed in bfloat16 or wider, within the bound.
A program may use at most 128 MiB of HBM per device.

v0:
```python
import math

import jax
import jax.numpy as jnp
from jax import lax
from jax.sharding import PartitionSpec as P

HEAD_DIM = 128
BLOCK = 128


neg_fill = -1e30


def shifted(block, axis, distance):
    devices = range(lax.axis_size(axis))
    route = [(i - distance, i) for i in devices if i - distance in devices]
    return lax.ppermute(block, axis, route)


def shards(queries, key_states, value_states, block_picks, out_weight, out_grad):
    query_rows = queries[0]
    key_rows = key_states[0]
    value_rows = value_states[0]
    grad_rows = out_grad[0]
    picks_here = block_picks[0]
    tok_count = query_rows.shape[0]
    q_cols = query_rows.shape[1]
    kv_cols = key_rows.shape[1]
    kv_count = kv_cols // HEAD_DIM
    group_size = q_cols // kv_cols
    score_scale = 1.0 / math.sqrt(HEAD_DIM)
    seq_count = lax.axis_size("seq")
    level_count = seq_count.bit_length() - 1
    shard_index = lax.axis_index("seq")
    far_keys = []
    far_values = []
    for level_index in range(level_count):
        distance = 1 << level_index
        got_keys, got_values = shifted((key_rows, value_rows), "seq", distance)
        row_begin = picks_here[level_index, shard_index] * BLOCK
        far_keys.append(lax.dynamic_slice_in_dim(got_keys, row_begin, BLOCK, 0))
        far_values.append(lax.dynamic_slice_in_dim(got_values, row_begin, BLOCK, 0))
    all_keys = jnp.concatenate([key_rows] + far_keys, 0)
    all_values = jnp.concatenate([value_rows] + far_values, 0)
    key_total = all_keys.shape[0]
    row_ids = lax.broadcasted_iota(jnp.int32, (tok_count, key_total), 0)
    col_ids = lax.broadcasted_iota(jnp.int32, (tok_count, key_total), 1)
    far_level = jnp.maximum(col_ids - tok_count, 0) // BLOCK
    far_seen = shard_index >= jnp.left_shift(jnp.int32(1), far_level)
    visible = jnp.where(col_ids < tok_count, col_ids <= row_ids, far_seen)
    whole_weight = lax.all_gather(out_weight, ("dp", "seq"), axis=0, tiled=True)
    attn_grad = lax.dot_general(
        grad_rows, whole_weight, (((1,), (1,)), ((), ())), preferred_element_type=jnp.float32
    )
    attn_grad = attn_grad.astype(jnp.bfloat16)
    query_heads = query_rows.reshape(tok_count, kv_count, group_size, HEAD_DIM)
    key_heads = all_keys.reshape(key_total, kv_count, HEAD_DIM)
    value_heads = all_values.reshape(key_total, kv_count, HEAD_DIM)
    grad_heads = attn_grad.reshape(tok_count, kv_count, group_size, HEAD_DIM)
    attn_parts = []
    dq_parts = []
    dk_parts = []
    dv_parts = []
    for group_index in range(kv_count):
        query_group = query_heads[:, group_index]
        key_group = key_heads[:, group_index]
        value_group = value_heads[:, group_index]
        grad_group = grad_heads[:, group_index]
        scores = (
            jnp.einsum("tgd,sd->gts", query_group, key_group, preferred_element_type=jnp.float32)
            * score_scale
        )
        scores = jnp.where(visible[None], scores, neg_fill)
        row_max = jnp.max(scores, axis=-1, keepdims=True)
        exp_scores = jnp.exp(scores - row_max)
        probs = exp_scores / jnp.sum(exp_scores, axis=-1, keepdims=True)
        probs_low = probs.astype(jnp.bfloat16)
        attn_group = jnp.einsum(
            "gts,sd->tgd", probs_low, value_group, preferred_element_type=jnp.float32
        ).astype(jnp.bfloat16)
        row_delta = jnp.einsum(
            "tgd,tgd->gt", grad_group, attn_group, preferred_element_type=jnp.float32
        )[:, :, None]
        prob_grad = jnp.einsum(
            "tgd,sd->gts", grad_group, value_group, preferred_element_type=jnp.float32
        )
        score_low = (probs * (prob_grad - row_delta)).astype(jnp.bfloat16)
        dq_parts.append(
            (
                jnp.einsum("gts,sd->tgd", score_low, key_group, preferred_element_type=jnp.float32)
                * score_scale
            ).astype(jnp.bfloat16)
        )
        dk_parts.append(
            jnp.einsum("gts,tgd->sd", score_low, query_group, preferred_element_type=jnp.float32)
            * score_scale
        )
        dv_parts.append(
            jnp.einsum("gts,tgd->sd", probs_low, grad_group, preferred_element_type=jnp.float32)
        )
        attn_parts.append(attn_group)
    attn_all = jnp.stack(attn_parts, 1).reshape(tok_count, q_cols)
    query_grad = jnp.stack(dq_parts, 1).reshape(tok_count, q_cols)
    key_terms = jnp.stack(dk_parts, 1).reshape(key_total, kv_cols)
    value_terms = jnp.stack(dv_parts, 1).reshape(key_total, kv_cols)
    layer_sum = jnp.dot(attn_all, whole_weight, preferred_element_type=jnp.float32)
    layer_out = layer_sum.astype(jnp.bfloat16)
    key_grad = key_terms[:tok_count]
    value_grad = value_terms[:tok_count]
    for level_index in range(level_count):
        distance = 1 << level_index
        begin = tok_count + level_index * BLOCK
        back_keys, back_values = shifted(
            (key_terms[begin : begin + BLOCK], value_terms[begin : begin + BLOCK]), "seq", -distance
        )
        source = jnp.minimum(shard_index + distance, seq_count - 1)
        row_begin = picks_here[level_index, source] * BLOCK
        key_grad = lax.dynamic_update_slice_in_dim(
            key_grad,
            lax.dynamic_slice_in_dim(key_grad, row_begin, BLOCK, 0) + back_keys,
            row_begin,
            0,
        )
        value_grad = lax.dynamic_update_slice_in_dim(
            value_grad,
            lax.dynamic_slice_in_dim(value_grad, row_begin, BLOCK, 0) + back_values,
            row_begin,
            0,
        )
    return (
        layer_out[None],
        query_grad[None],
        key_grad.astype(jnp.bfloat16)[None],
        value_grad.astype(jnp.bfloat16)[None],
    )


def solution(mesh):
    return jax.shard_map(
        shards,
        mesh=mesh,
        in_specs=(
            P("dp", "seq", None),
            P("dp", "seq", None),
            P("dp", "seq", None),
            P("dp", None, None),
            P(("dp", "seq"), None),
            P("dp", "seq", None),
        ),
        out_specs=(
            P("dp", "seq", None),
            P("dp", "seq", None),
            P("dp", "seq", None),
            P("dp", "seq", None),
        ),
        check_vma=False,
    )
```

profile of v0, /device:TPU:0, one launch (start us, length us, event | category | flops | bytes accessed | tf_op | source)
XLA Modules:
  0.0 234.0 jit_solution(6987228526842534962)
XLA Ops:
  9.0 6.0 %collective-permute-start.5 = (bf16[256,512]{0,1:T(8,128)(2,1)S(1)}, bf16[256,512]{0,1:T(8,128)(2,1)S(1)}, u32[]{:S(2)}, u32[]{:S(2)}) collective-permute-start(bf16[256,512]{0,1:T(8,128)(2,1)S(1)} %bitcast.364), channel_id=1, source_target_pairs={{0,4},{1,5},{2,6},{3,7},{8,12},{9,13},{10,14},{11,15},{16,20},{17,... | collective-permute-start | bytes 786440 | tf_op jit(solution)/shard_map/ppermute | solution.py:18
  15.0 4.2 %collective-permute-start.4 = (bf16[256,512]{0,1:T(8,128)(2,1)S(1)}, bf16[256,512]{0,1:T(8,128)(2,1)}, u32[]{:S(2)}, u32[]{:S(2)}) collective-permute-start(bf16[256,512]{0,1:T(8,128)(2,1)S(1)} %bitcast.365), channel_id=1, source_target_pairs={{0,2},{1,3},{2,4},{3,5},{4,6},{5,7},{8,10},{9,11},{10,12},{11,13},... | collective-permute-start | bytes 786440 | tf_op jit(solution)/shard_map/ppermute | solution.py:18
  19.2 3.4 %collective-permute-start.3 = (bf16[256,512]{0,1:T(8,128)(2,1)S(1)}, bf16[256,512]{0,1:T(8,128)(2,1)S(1)}, u32[]{:S(2)}, u32[]{:S(2)}) collective-permute-start(bf16[256,512]{0,1:T(8,128)(2,1)S(1)} %bitcast.366), channel_id=1, source_target_pairs={{0,1},{1,2},{2,3},{3,4},{4,5},{5,6},{6,7},{8,9},{9,10},{10,11},{11... | collective-permute-start | bytes 786440 | tf_op jit(solution)/shard_map/ppermute | solution.py:18
  35.9 2.6 %collective-permute-start = (bf16[256,512]{1,0:T(8,128)(2,1)}, bf16[256,512]{1,0:T(8,128)(2,1)}, u32[]{:S(2)}, u32[]{:S(2)}) collective-permute-start(bf16[256,512]{1,0:T(8,128)(2,1)} %bitcast.9), channel_id=1, source_target_pairs={{0,1},{1,2},{2,3},{3,4},{4,5},{5,6},{6,7},{8,9},{9,10},{10,11},{11... | collective-permute-start | bytes 786440 | tf_op jit(solution)/shard_map/ppermute | solution.py:18
  48.6 2.5 %fusion.92 = (f32[4,256]{1,0:T(4,128)S(1)}, f32[4,256,640]{1,2,0:T(8,128)}) fusion(pred[256,640]{0,1:T(8,128)(4,1)S(1)} %copy-done.44, bf16[256,4,4,128]{0,3,2,1:T(8,128)(2,1)S(1)} %bitcast.353, bf16[640,4,128]{2,0,1:T(8,128)(2,1)S(1)} %pad_maximum_fusion.5), kind=kOutput, calls=%fused_computation.181 | convolution fusion | flops 170394240 | bytes 3215360 | tf_op jit(solution)/shard_map/sub | solution.py:76
  51.1 2.4 %fusion.93 = (f32[4,256]{1,0:T(4,128)S(1)}, f32[4,256,640]{1,2,0:T(8,128)}) fusion(pred[256,640]{0,1:T(8,128)(4,1)S(1)} %copy-done.44, bf16[256,4,4,128]{0,3,2,1:T(8,128)(2,1)S(1)} %bitcast.354, bf16[640,4,128]{2,0,1:T(8,128)(2,1)S(1)} %pad_maximum_fusion.5), kind=kOutput, calls=%fused_computation.182 | convolution fusion | flops 170394240 | bytes 3215360 | tf_op jit(solution)/shard_map/sub | solution.py:76
  53.5 2.5 %fusion.90 = (f32[4,256]{1,0:T(4,128)S(1)}, f32[4,256,640]{1,2,0:T(8,128)}) fusion(pred[256,640]{0,1:T(8,128)(4,1)S(1)} %copy-done.44, bf16[256,4,4,128]{0,3,2,1:T(8,128)(2,1)S(1)} %bitcast.355, bf16[640,4,128]{2,0,1:T(8,128)(2,1)S(1)} %pad_maximum_fusion.5), kind=kOutput, calls=%fused_computation.179 | convolution fusion | flops 170394240 | bytes 3215360 | tf_op jit(solution)/shard_map/sub | solution.py:76
  56.1 2.5 %fusion.91 = (f32[4,256]{1,0:T(4,128)S(1)}, f32[4,256,640]{1,2,0:T(8,128)}) fusion(pred[256,640]{0,1:T(8,128)(4,1)S(1)} %copy-done.44, bf16[256,4,4,128]{0,3,2,1:T(8,128)(2,1)S(1)} %bitcast.356, bf16[640,4,128]{2,0,1:T(8,128)(2,1)S(1)} %pad_maximum_fusion.5), kind=kOutput, calls=%fused_computation.180 | convolution fusion | flops 170394240 | bytes 3215360 | tf_op jit(solution)/shard_map/sub | solution.py:76
  58.5 3.2 %fusion.46 = bf16[4,256,640]{1,2,0:T(8,128)(2,1)} fusion(f32[4,256,640]{1,2,0:T(8,128)} %get-tuple-element.33, f32[4,256]{1,0:T(4,128)S(1)} %get-tuple-element.32), kind=kLoop, calls=%fused_computation.82 | loop fusion | flops 1310720 | bytes 3936256 | tf_op jit(solution)/shard_map/convert_element_type | solution.py:78
  66.4 39.2 %all-gather.2.cloned.1.call-done = bf16[2048,2048]{1,0:T(8,128)(2,1)} async-done(((bf16[64,2048]{1,0:T(8,128)(2,1)}), bf16[2048,2048]{1,0:T(8,128)(2,1)}) %all-gather.2.cloned.1.call-update) | async-done | bytes 8388624 | tf_op jit(solution)/shard_map/all_gather | solution.py:52
  105.6 6.7 %convolution_convert_fusion = bf16[256,2048]{1,0:T(8,128)(2,1)} fusion(bf16[2048,2048]{1,0:T(8,128)(2,1)} %all-gather.2.cloned.1.call-done, bf16[1,256,2048]{2,1,0:T(8,128)(2,1)S(1)} %copy-done), kind=kOutput, calls=%fused_computation.24 | convolution fusion | flops 2148007936 | bytes 10485760 | tf_op jit(solution)/shard_map/dot_general | solution.py:53
  116.5 2.1 copy.142
  118.7 2.8 %convolution_bitcast_fusion.2 = f32[640,1,128]{0,2,1:T(8,128)} fusion(bf16[4,256,640]{1,2,0:T(8,128)(2,1)} %fusion.46, bf16[256,1,4,128]{3,2,1,0:T(4,128)(2,1)} %copy-done.27), kind=kOutput, calls=%fused_computation.63 | convolution fusion | flops 167772160 | bytes 1900544 | tf_op jit(solution)/shard_map/gts,tgd->sd/dot_general | solution.py:100
  129.6 2.8 %convolution_bitcast_fusion.3 = f32[640,1,128]{0,2,1:T(8,128)} fusion(bf16[4,256,640]{1,2,0:T(8,128)(2,1)} %fusion.45, bf16[256,1,4,128]{3,2,1,0:T(4,128)(2,1)} %copy-done.26), kind=kOutput, calls=%fused_computation.64 | convolution fusion | flops 167772160 | bytes 1900544 | tf_op jit(solution)/shard_map/gts,tgd->sd/dot_general | solution.py:100
  132.4 2.2 multiply_reduce_fusion.3
  142.6 2.8 %convolution_bitcast_fusion = f32[640,1,128]{0,2,1:T(8,128)} fusion(bf16[4,256,640]{1,2,0:T(8,128)(2,1)} %fusion.48, bf16[256,1,4,128]{3,2,1,0:T(4,128)(2,1)} %get-tuple-element.21), kind=kOutput, calls=%fused_computation.61 | convolution fusion | flops 167772160 | bytes 1900544 | tf_op jit(solution)/shard_map/gts,tgd->sd/dot_general | solution.py:100
  145.4 2.2 multiply_reduce_fusion
  154.6 2.4 %convolution_bitcast_fusion.1 = f32[640,1,128]{0,2,1:T(8,128)} fusion(bf16[4,256,640]{1,2,0:T(8,128)(2,1)S(1)} %fusion.47, bf16[256,1,4,128]{3,2,1,0:T(4,128)(2,1)} %get-tuple-element.19), kind=kOutput, calls=%fused_computation.62 | convolution fusion | flops 167772160 | bytes 1900544 | tf_op jit(solution)/shard_map/gts,tgd->sd/dot_general | solution.py:100
  157.0 2.2 multiply_reduce_fusion.1
  171.0 6.7 %fusion.12 = bf16[1,256,2048]{2,1,0:T(8,128)(2,1)} fusion(bf16[256,2048]{0,1:T(8,128)(2,1)S(1)} %bitcast.351, bf16[2048,2048]{1,0:T(8,128)(2,1)} %all-gather.2.cloned.1.call-done), kind=kOutput, calls=%fused_computation.26 | convolution fusion | flops 2148007936 | bytes 10485760 | tf_op jit(solution)/shard_map/dot_general | solution.py:107
  190.7 6.3 %collective-permute-done.7 = f32[128,512]{1,0:T(8,128)} collective-permute-done((f32[128,512]{1,0:T(8,128)}, f32[128,512]{1,0:T(8,128)}, u32[]{:S(2)}, u32[]{:S(2)}) %collective-permute-start.7) | collective-permute-done | bytes 262176 | tf_op jit(solution)/shard_map/ppermute | solution.py:18
  198.1 5.3 %collective-permute-done.10 = f32[128,512]{1,0:T(8,128)S(1)} collective-permute-done((f32[128,512]{1,0:T(8,128)S(1)}, f32[128,512]{1,0:T(8,128)S(1)}, u32[]{:S(2)}, u32[]{:S(2)}) %collective-permute-start.10) | collective-permute-done | bytes 262176 | tf_op jit(solution)/shard_map/ppermute | solution.py:18
  203.5 8.4 %collective-permute-done.8 = f32[128,512]{1,0:T(8,128)} collective-permute-done((f32[128,512]{1,0:T(8,128)S(1)}, f32[128,512]{1,0:T(8,128)}, u32[]{:S(2)}, u32[]{:S(2)}) %collective-permute-start.8) | collective-permute-done | bytes 262176 | tf_op jit(solution)/shard_map/ppermute | solution.py:18
  213.6 12.8 %collective-permute-done.11 = f32[128,512]{1,0:T(8,128)S(1)} collective-permute-done((f32[128,512]{1,0:T(8,128)S(1)}, f32[128,512]{1,0:T(8,128)S(1)}, u32[]{:S(2)}, u32[]{:S(2)}) %collective-permute-start.11) | collective-permute-done | bytes 262176 | tf_op jit(solution)/shard_map/ppermute | solution.py:18
  (180 shorter events, 81.2 us)
Async XLA Ops:
  7.2 98.5 %copy-start = (bf16[1,256,2048]{2,1,0:T(8,128)(2,1)S(1)}, bf16[1,256,2048]{2,1,0:T(8,128)(2,1)}, u32[]{:S(2)}) copy-start(bf16[1,256,2048]{2,1,0:T(8,128)(2,1)} %param.11) | copy-start | bytes 3145732
  7.2 98.4 %all-gather.2.cloned.1.call-start = ((), (), s32[]{:S(2)}) async-start(), calls=%async_computation | async-start | bytes 8650752 | tf_op jit(solution)/shard_map/all_gather | solution.py:52
  9.0 26.9 %collective-permute-start.5 = (bf16[256,512]{0,1:T(8,128)(2,1)S(1)}, bf16[256,512]{0,1:T(8,128)(2,1)S(1)}, u32[]{:S(2)}, u32[]{:S(2)}) collective-permute-start(bf16[256,512]{0,1:T(8,128)(2,1)S(1)} %bitcast.364), channel_id=1, source_target_pairs={{0,4},{1,5},{2,6},{3,7},{8,12},{9,13},{10,14},{11,15},{16,20},{17,... | collective-permute-start | bytes 786440 | tf_op jit(solution)/shard_map/ppermute | solution.py:18
  15.0 23.6 %collective-permute-start.4 = (bf16[256,512]{0,1:T(8,128)(2,1)S(1)}, bf16[256,512]{0,1:T(8,128)(2,1)}, u32[]{:S(2)}, u32[]{:S(2)}) collective-permute-start(bf16[256,512]{0,1:T(8,128)(2,1)S(1)} %bitcast.365), channel_id=1, source_target_pairs={{0,2},{1,3},{2,4},{3,5},{4,6},{5,7},{8,10},{9,11},{10,12},{11,13},... | collective-permute-start | bytes 786440 | tf_op jit(solution)/shard_map/ppermute | solution.py:18
  19.2 20.3 %collective-permute-start.3 = (bf16[256,512]{0,1:T(8,128)(2,1)S(1)}, bf16[256,512]{0,1:T(8,128)(2,1)S(1)}, u32[]{:S(2)}, u32[]{:S(2)}) collective-permute-start(bf16[256,512]{0,1:T(8,128)(2,1)S(1)} %bitcast.366), channel_id=1, source_target_pairs={{0,1},{1,2},{2,3},{3,4},{4,5},{5,6},{6,7},{8,9},{9,10},{10,11},{11... | collective-permute-start | bytes 786440 | tf_op jit(solution)/shard_map/ppermute | solution.py:18
  22.6 18.0 %collective-permute-start.2 = (bf16[256,512]{1,0:T(8,128)(2,1)}, bf16[256,512]{1,0:T(8,128)(2,1)}, u32[]{:S(2)}, u32[]{:S(2)}) collective-permute-start(bf16[256,512]{1,0:T(8,128)(2,1)} %bitcast.9), channel_id=1, source_target_pairs={{0,4},{1,5},{2,6},{3,7},{8,12},{9,13},{10,14},{11,15},{16,20},{17,... | collective-permute-start | bytes 786440 | tf_op jit(solution)/shard_map/ppermute | solution.py:18
  24.6 18.5 %collective-permute-start.1 = (bf16[256,512]{1,0:T(8,128)(2,1)}, bf16[256,512]{1,0:T(8,128)(2,1)}, u32[]{:S(2)}, u32[]{:S(2)}) collective-permute-start(bf16[256,512]{1,0:T(8,128)(2,1)} %bitcast.9), channel_id=1, source_target_pairs={{0,2},{1,3},{2,4},{3,5},{4,6},{5,7},{8,10},{9,11},{10,12},{11,13},... | collective-permute-start | bytes 786440 | tf_op jit(solution)/shard_map/ppermute | solution.py:18
  35.9 20.2 %copy-start.4 = (bf16[1,256,2048]{1,2,0:T(8,128)(2,1)}, bf16[1,256,2048]{1,2,0:T(8,128)(2,1)S(1)}, u32[]{:S(2)}) copy-start(bf16[1,256,2048]{1,2,0:T(8,128)(2,1)S(1)} %copy.71) | copy-start | bytes 3145732
  35.9 8.8 %collective-permute-start = (bf16[256,512]{1,0:T(8,128)(2,1)}, bf16[256,512]{1,0:T(8,128)(2,1)}, u32[]{:S(2)}, u32[]{:S(2)}) collective-permute-start(bf16[256,512]{1,0:T(8,128)(2,1)} %bitcast.9), channel_id=1, source_target_pairs={{0,1},{1,2},{2,3},{3,4},{4,5},{5,6},{6,7},{8,9},{9,10},{10,11},{11... | collective-permute-start | bytes 786440 | tf_op jit(solution)/shard_map/ppermute | solution.py:18
  47.5 8.6 %copy-start.22 = (bf16[640,4,128]{2,0,1:T(8,128)(2,1)}, bf16[640,4,128]{2,0,1:T(8,128)(2,1)S(1)}, u32[]{:S(2)}) copy-start(bf16[640,4,128]{2,0,1:T(8,128)(2,1)S(1)} %pad_maximum_fusion.5) | copy-start | bytes 1966084
  116.5 5.0 %copy-start.13 = (bf16[640,4,128]{0,2,1:T(8,128)(2,1)S(1)}, bf16[640,4,128]{0,2,1:T(8,128)(2,1)}, u32[]{:S(2)}) copy-start(bf16[640,4,128]{0,2,1:T(8,128)(2,1)} %pad_maximum_fusion.4) | copy-start | bytes 1966084
  116.5 7.1 %copy-start.28 = (bf16[256,1,4,128]{3,2,1,0:T(4,128)(2,1)S(1)}, bf16[256,1,4,128]{3,2,1,0:T(4,128)(2,1)}, u32[]{:S(2)}) copy-start(bf16[256,1,4,128]{3,2,1,0:T(4,128)(2,1)} %copy-done.27) | copy-start | bytes 786436
  129.6 5.1 %copy-start.20 = (f32[4,256,640]{1,2,0:T(8,128)S(1)}, f32[4,256,640]{1,2,0:T(8,128)}, u32[]{:S(2)}) copy-start(f32[4,256,640]{1,2,0:T(8,128)} %get-tuple-element.35) | copy-start | bytes 7864324
  142.6 5.0 %copy-start.18 = (f32[4,256,640]{1,2,0:T(8,128)S(1)}, f32[4,256,640]{1,2,0:T(8,128)}, u32[]{:S(2)}) copy-start(f32[4,256,640]{1,2,0:T(8,128)} %get-tuple-element.29) | copy-start | bytes 7864324
  165.3 5.5 %copy-start.29 = (bf16[128,4,256]{2,0,1:T(8,128)(2,1)S(1)}, bf16[128,4,256]{2,0,1:T(8,128)(2,1)}, u32[]{:S(2)}) copy-start(bf16[128,4,256]{2,0,1:T(8,128)(2,1)} %get-tuple-element.41) | copy-start | bytes 786436
  165.3 5.5 %copy-start.30 = (bf16[128,4,256]{2,0,1:T(8,128)(2,1)S(1)}, bf16[128,4,256]{2,0,1:T(8,128)(2,1)}, u32[]{:S(2)}) copy-start(bf16[128,4,256]{2,0,1:T(8,128)(2,1)} %get-tuple-element.43) | copy-start | bytes 786436
  165.3 5.5 %copy-start.31 = (bf16[128,4,256]{2,0,1:T(8,128)(2,1)S(1)}, bf16[128,4,256]{2,0,1:T(8,128)(2,1)}, u32[]{:S(2)}) copy-start(bf16[128,4,256]{2,0,1:T(8,128)(2,1)} %get-tuple-element.37) | copy-start | bytes 786436
  165.3 5.5 %copy-start.32 = (bf16[128,4,256]{2,0,1:T(8,128)(2,1)S(1)}, bf16[128,4,256]{2,0,1:T(8,128)(2,1)}, u32[]{:S(2)}) copy-start(bf16[128,4,256]{2,0,1:T(8,128)(2,1)} %get-tuple-element.39) | copy-start | bytes 786436
  165.3 22.1 %collective-permute-start.6 = (f32[128,512]{1,0:T(8,128)}, f32[128,512]{1,0:T(8,128)}, u32[]{:S(2)}, u32[]{:S(2)}) collective-permute-start(f32[128,512]{1,0:T(8,128)} %copy.105), channel_id=1, source_target_pairs={{1,0},{2,1},{3,2},{4,3},{5,4},{6,5},{7,6},{9,8},{10,9},{11,10},{12... | collective-permute-start | bytes 786440 | tf_op jit(solution)/shard_map/ppermute | solution.py:18
  169.5 20.2 %collective-permute-start.9 = (f32[128,512]{1,0:T(8,128)}, f32[128,512]{1,0:T(8,128)}, u32[]{:S(2)}, u32[]{:S(2)}) collective-permute-start(f32[128,512]{1,0:T(8,128)} %copy.118), channel_id=1, source_target_pairs={{1,0},{2,1},{3,2},{4,3},{5,4},{6,5},{7,6},{9,8},{10,9},{11,10},{12... | collective-permute-start | bytes 786440 | tf_op jit(solution)/shard_map/ppermute | solution.py:18
  182.9 14.2 %collective-permute-start.7 = (f32[128,512]{1,0:T(8,128)}, f32[128,512]{1,0:T(8,128)}, u32[]{:S(2)}, u32[]{:S(2)}) collective-permute-start(f32[128,512]{1,0:T(8,128)} %copy.107), channel_id=1, source_target_pairs={{2,0},{3,1},{4,2},{5,3},{6,4},{7,5},{10,8},{11,9},{12,10},{13,11},... | collective-permute-start | bytes 786440 | tf_op jit(solution)/shard_map/ppermute | solution.py:18
  184.3 27.6 %collective-permute-start.8 = (f32[128,512]{1,0:T(8,128)S(1)}, f32[128,512]{1,0:T(8,128)}, u32[]{:S(2)}, u32[]{:S(2)}) collective-permute-start(f32[128,512]{1,0:T(8,128)S(1)} %copy.108), channel_id=1, source_target_pairs={{4,0},{5,1},{6,2},{7,3},{12,8},{13,9},{14,10},{15,11},{20,16},{21,... | collective-permute-start | bytes 786440 | tf_op jit(solution)/shard_map/ppermute | solution.py:18
  186.1 17.3 %collective-permute-start.10 = (f32[128,512]{1,0:T(8,128)S(1)}, f32[128,512]{1,0:T(8,128)S(1)}, u32[]{:S(2)}, u32[]{:S(2)}) collective-permute-start(f32[128,512]{1,0:T(8,128)S(1)} %copy.120), channel_id=1, source_target_pairs={{2,0},{3,1},{4,2},{5,3},{6,4},{7,5},{10,8},{11,9},{12,10},{13,11},... | collective-permute-start | bytes 786440 | tf_op jit(solution)/shard_map/ppermute | solution.py:18
  187.4 39.0 %collective-permute-start.11 = (f32[128,512]{1,0:T(8,128)S(1)}, f32[128,512]{1,0:T(8,128)S(1)}, u32[]{:S(2)}, u32[]{:S(2)}) collective-permute-start(f32[128,512]{1,0:T(8,128)S(1)} %copy.121), channel_id=1, source_target_pairs={{4,0},{5,1},{6,2},{7,3},{12,8},{13,9},{14,10},{15,11},{20,16},{21,... | collective-permute-start | bytes 786440 | tf_op jit(solution)/shard_map/ppermute | solution.py:18
  (36 other events, 82.2 us)
Sparse Core Ops, SparseCore 0:
  11.0 94.5 all-gather.1
where the time goes:
time: 235 us; the launch traced here: 234 us
  waiting for transfers between devices  73.5 us (31%)
  matrix products  59.8 us (25%)
  local copies, waits for them, and re-layouts  32.5 us (14%)
  starting transfers between devices  28.3 us (12%)
  other arithmetic  21.5 us (9%)
  between operations  18.4 us (8%)
    all_gather x1, waiting for transfers between devices, shards(): whole_weight = lax.all_gather(out_weight, ('dp', 'seq'), axis=0, tiled=True)  39.2 us
    ppermute x12, waiting for transfers between devices, shifted(): return lax.ppermute(block, axis, route)  33.7 us
    ppermute x12, starting transfers between devices, shifted(): return lax.ppermute(block, axis, route)  28.2 us
    unnamed x98, local copies, waits for them, and re-layouts  16.7 us
    dot_general x4, matrix products, shards(): jnp.einsum('gts,tgd->sd', probs_low, grad_group, preferred_element_type=j...  10.9 us
    sub x4, matrix products, shards(): exp_scores = jnp.exp(scores - row_max)  9.91 us
    dot_general x4, matrix products, shards(): jnp.einsum('gts,sd->tgd', probs_low, value_group, preferred_element_type=...  8.71 us
    dot_general x4, matrix products, shards(): jnp.einsum('gts,sd->tgd', score_low, key_group, preferred_element_type=jn...  8.28 us
  transfers between devices with their start and end apart: 13, of which 6 were waited for; matrix products, arithmetic and copies ran while one was open for 21% of the time, Pallas kernels for 0%

commit v1 on v0

--- a/solution.py
+++ b/solution.py
@@ -3,6 +3,8 @@
 import jax
 import jax.numpy as jnp
 from jax import lax
+from jax.experimental import pallas as pl
+from jax.experimental.pallas import tpu as pltpu
 from jax.sharding import PartitionSpec as P
 
 HEAD_DIM = 128
@@ -136,9 +138,415 @@
     )
 
 
+MESH = pl.DeviceIdType.MESH
+NT = (((1,), (1,)), ((), ()))
+NN = (((1,), (0,)), ((), ()))
+TN = (((0,), (0,)), ((), ()))
+
+
+def dot(a, b, dims):
+    return lax.dot_general(a, b, dims, preferred_element_type=jnp.float32)
+
+
+def fused_kernel(
+    picks, q_hbm, k_in, v_in, w_in, og_hbm,
+    lo_out, dq_out, dk_out, dv_out,
+    q_v, og_v, wbuf, kall, vall, k_t, v_t, kv_stage, probs, attn_t, lo_acc,
+    dk_acc, dv_acc, gr_stage, gr_in,
+    in_sem, kv_ssem, kv_rsem, z_ssem, x_ssem, y_ssem, s_ssem, xh_ssem, yh_ssem,
+    z_rsem, x_rsem, y_rsem, s_rsem, xh_rsem, yh_rsem, gr_ssem, gr_rsem,
+):
+    dp = lax.axis_index("dp")
+    seq = lax.axis_index("seq")
+    n_seq = lax.axis_size("seq")
+    n_z = n_seq // 2
+    x, core = dp // 2, dp % 2
+    z, y = seq // 2, seq % 2
+    rows = w_in.shape[0]
+    half = rows // 2
+    tok = q_v.shape[0]
+    group_rows = rows * n_seq
+    pair_rows = group_rows // 2
+    heads = q_v.shape[1] // HEAD_DIM
+    kv_heads = k_in.shape[1] // HEAD_DIM
+    group_size = heads // kv_heads
+    pair_heads = group_size // 2
+    levels = n_seq.bit_length() - 1
+    scale = 1.0 / math.sqrt(HEAD_DIM)
+    log2_scale = scale * math.log2(math.e)
+
+    sib = (x * 2 + 1 - core, seq)
+    xn = ((1 - x) * 2 + core, seq)
+    yn = (dp, z * 2 + 1 - y)
+    d_own, d_sib, d_x, d_xs = dp, sib[0], xn[0], (1 - x) * 2 + 1 - core
+
+    q_copy = pltpu.make_async_copy(q_hbm, q_v, in_sem.at[0])
+    og_copy = pltpu.make_async_copy(og_hbm, og_v, in_sem.at[1])
+    q_copy.start()
+    og_copy.start()
+
+    barrier = pltpu.get_barrier_semaphore()
+    count = jnp.int32(2)
+    for dev in (sib, xn):
+        pl.semaphore_signal(barrier, inc=1, device_id=dev, device_id_type=MESH)
+    for j in range(levels):
+        dist = 1 << j
+
+        @pl.when(seq + dist < n_seq)
+        def _():
+            pl.semaphore_signal(barrier, inc=1, device_id=(dp, seq + dist), device_id_type=MESH)
+
+        @pl.when(seq >= dist)
+        def _():
+            pl.semaphore_signal(barrier, inc=1, device_id=(dp, seq - dist), device_id_type=MESH)
+
+        count += (seq + dist < n_seq).astype(jnp.int32) + (seq >= dist).astype(jnp.int32)
+
+    def w_row(d, zz, yy):
+        return pl.multiple_of((d * n_seq + zz * 2 + yy) * rows, rows)
+
+    def w_at(d, zz, yy):
+        return wbuf.at[pl.ds(w_row(d, zz, yy), rows)]
+
+    def w_half(d, zz, yy, hf):
+        return wbuf.at[pl.ds(pl.multiple_of(w_row(d, zz, yy) + hf * half, half), half)]
+
+    for j in range(levels):
+        target = jnp.minimum(seq + (1 << j), n_seq - 1)
+        second = picks[0, j, target].astype(jnp.float32)
+        for i, buf in enumerate((k_in, v_in)):
+            first_rows = buf[0:BLOCK, :].astype(jnp.float32) * (1.0 - second)
+            second_rows = buf[BLOCK : 2 * BLOCK, :].astype(jnp.float32) * second
+            kv_stage[j, i] = (first_rows + second_rows).astype(jnp.bfloat16)
+    wbuf[pl.ds(w_row(dp, z, y), rows), :] = w_in[...]
+    kall[0:tok, :] = k_in[...]
+    vall[0:tok, :] = v_in[...]
+    pl.semaphore_wait(barrier, count)
+
+    def remote(src, dst, ssem, rsem, dev):
+        return pltpu.make_async_remote_copy(
+            src_ref=src, dst_ref=dst, send_sem=ssem, recv_sem=rsem, device_id=dev, device_id_type=MESH
+        )
+
+    def kv_copies(j):
+        out = []
+        for i, buf in enumerate((kall, vall)):
+            dst = buf.at[pl.ds(tok + j * BLOCK, BLOCK)]
+            dev = (dp, jnp.minimum(seq + (1 << j), n_seq - 1))
+            out.append(remote(kv_stage.at[j, i], dst, kv_ssem.at[j, i], kv_rsem.at[j, i], dev))
+        return out
+
+    z_order = (z, jnp.bitwise_xor(z, 1), jnp.where(z < 2, 2, 1), jnp.where(z < 2, 3, 0))
+
+    def z_copy(zz, up):
+        dev = (dp, seq + 2) if up else (dp, seq - 2)
+        return remote(w_at(dp, zz, y), w_at(dp, zz, y), z_ssem.at[int(up), zz], z_rsem.at[zz], dev)
+
+    def x_copy(zz, d):
+        return remote(w_at(d, zz, y), w_at(d, zz, y), x_ssem.at[zz], x_rsem.at[zz], xn)
+
+    def y_copy(zz, yy):
+        return remote(w_at(dp, zz, yy), w_at(dp, zz, yy), y_ssem.at[zz], y_rsem.at[zz], yn)
+
+    def xh_copy(zz, d):
+        piece = w_half(d, zz, 1 - y, 1)
+        return remote(piece, piece, xh_ssem.at[zz], xh_rsem.at[zz], xn)
+
+    def yh_copy(zz, yy):
+        piece = w_half(d_x, zz, yy, 0)
+        return remote(piece, piece, yh_ssem.at[zz], yh_rsem.at[zz], yn)
+
+    def s_copy(zz, kind, other):
+        d = (d_x if kind & 1 else d_own) if not other else (d_xs if kind & 1 else d_sib)
+        yy = 1 - y if kind & 2 else y
+        piece = w_at(d, zz, yy)
+        return remote(piece, piece, s_ssem.at[kind, zz], s_rsem.at[kind, zz], sib)
+
+    def z_sends(zz, act):
+        @pl.when(jnp.logical_and(zz <= z, z < n_z - 1))
+        def _():
+            act(z_copy(zz, True))
+
+        @pl.when(jnp.logical_and(zz >= z, z > 0))
+        def _():
+            act(z_copy(zz, False))
+
+    def start(c):
+        c.start()
+
+    def own_event(i):
+        zz = z_order[i]
+        if i:
+            z_copy(zz, True).wait_recv()
+        z_sends(zz, start)
+        x_copy(zz, d_own).start()
+        y_copy(zz, y).start()
+        s_copy(zz, 0, False).start()
+
+    def xy_event(i):
+        zz = z_order[i]
+        x_copy(zz, d_x).wait_recv()
+        yh_copy(zz, y).start()
+        s_copy(zz, 1, False).start()
+        y_copy(zz, 1 - y).wait_recv()
+        xh_copy(zz, d_own).start()
+        s_copy(zz, 2, False).start()
+
+    def diag_event(i):
+        zz = z_order[i]
+        yh_copy(zz, 1 - y).wait_recv()
+        xh_copy(zz, d_x).wait_recv()
+        s_copy(zz, 3, False).start()
+
+    def sib_wait(i, kinds):
+        for kind in kinds:
+            s_copy(z_order[i], kind, True).wait_recv()
+
+    for j in range(levels):
+        @pl.when(seq + (1 << j) < n_seq)
+        def _():
+            for c in kv_copies(j):
+                c.start()
+
+    own_event(0)
+
+    for j in range(levels):
+        @pl.when(seq < (1 << j))
+        def _():
+            for buf in (kall, vall):
+                buf[tok + j * BLOCK : tok + (j + 1) * BLOCK, :] = jnp.zeros((BLOCK, buf.shape[1]), buf.dtype)
+
+    dk_acc[...] = jnp.zeros_like(dk_acc)
+    dv_acc[...] = jnp.zeros_like(dv_acc)
+    lo_acc[...] = jnp.zeros_like(lo_acc)
+    q_copy.wait()
+    for j in range(levels):
+        @pl.when(seq >= (1 << j))
+        def _():
+            for c in kv_copies(j):
+                c.wait_recv()
+
+    def group_cols(g):
+        return pl.ds(pl.multiple_of(g * HEAD_DIM, HEAD_DIM), HEAD_DIM)
+
+    causal = lax.broadcasted_iota(jnp.int32, (tok, tok), 0) <= lax.broadcasted_iota(jnp.int32, (tok, tok), 1)
+
+    def softmax_head(h, carry):
+        g = h // group_size
+        s = dot(kall[:, group_cols(g)], q_v[:, group_cols(h)], NT)
+        parts = [jnp.where(causal, s[:tok], neg_fill)]
+        for j in range(levels):
+            bias = jnp.where(seq >= (1 << j), 0.0, neg_fill).astype(jnp.float32)
+            parts.append(s[tok + j * BLOCK : tok + (j + 1) * BLOCK] + bias)
+        top = jnp.max(parts[0], axis=0, keepdims=True)
+        for part in parts[1:]:
+            top = jnp.maximum(top, jnp.max(part, axis=0, keepdims=True))
+        exps = [jnp.exp2((part - top) * log2_scale) for part in parts]
+        total = jnp.sum(exps[0], axis=0, keepdims=True)
+        for part in exps[1:]:
+            total = total + jnp.sum(part, axis=0, keepdims=True)
+        inv = 1.0 / total
+        low = jnp.concatenate([(part * inv).astype(jnp.bfloat16) for part in exps], 0)
+        probs[h] = low
+        at = dot(v_t[group_cols(g), :], low, NN)
+        attn_t[pl.ds(pl.multiple_of(h * HEAD_DIM, HEAD_DIM), HEAD_DIM), :] = at.astype(jnp.bfloat16)
+        return carry
+
+    k_t[...] = kall[...].T
+    v_t[...] = vall[...].T
+
+    def softmaxes(lo, hi):
+        lax.fori_loop(lo, hi, softmax_head, 0)
+
+    def unit(g, p):
+        base = pl.multiple_of(g * group_rows + p * pair_rows, pair_rows)
+        wp = wbuf[pl.ds(base, pair_rows), :]
+        g_t = dot(wp, og_v[...], NT).astype(jnp.bfloat16)
+        a_t = attn_t[pl.ds(base, pair_rows), :]
+        lo_acc[...] += dot(a_t, wp, TN)
+        cols = group_cols(g)
+        dk = dk_acc[g]
+        dv = dv_acc[g]
+        for i in range(pair_heads):
+            h = g * group_size + p * pair_heads + i
+            gh = g_t[i * HEAD_DIM : (i + 1) * HEAD_DIM]
+            ah = a_t[i * HEAD_DIM : (i + 1) * HEAD_DIM]
+            delta = jnp.sum(gh.astype(jnp.float32) * ah.astype(jnp.float32), axis=0, keepdims=True)
+            low = probs[h]
+            dprob = dot(vall[:, cols], gh, NN)
+            ds = (low.astype(jnp.float32) * (dprob - delta)).astype(jnp.bfloat16)
+            dq_t = dot(k_t[cols, :], ds, NN) * scale
+            dq_out[:, group_cols(h)] = dq_t.T.astype(jnp.bfloat16)
+            dk += dot(ds, q_v[:, group_cols(h)], NN)
+            dv += dot(low, gh, NT)
+        dk_acc[g] = dk
+        dv_acc[g] = dv
+
+    def gr_copy(g, j, back):
+        dev = (dp, jnp.maximum(seq - (1 << j), 0))
+        return remote(gr_stage.at[g, j], gr_in.at[g, j], gr_ssem.at[g, j], gr_rsem.at[g, j], dev)
+
+    def send_grads(g):
+        for j in range(levels):
+            @pl.when(seq >= (1 << j))
+            def _():
+                begin = tok + j * BLOCK
+                gr_stage[g, j, 0] = (dk_acc[g, begin : begin + BLOCK, :] * scale).astype(jnp.bfloat16)
+                gr_stage[g, j, 1] = dv_acc[g, begin : begin + BLOCK, :].astype(jnp.bfloat16)
+                gr_copy(g, j, True).start()
+
+    def finish_grads(g):
+        cols = group_cols(g)
+        for j in range(levels):
+            @pl.when(seq + (1 << j) < n_seq)
+            def _():
+                gr_copy(g, j, True).wait_recv()
+                second = picks[0, j, jnp.minimum(seq + (1 << j), n_seq - 1)].astype(jnp.float32)
+                for b, here in enumerate((1.0 - second, second)):
+                    part = slice(b * BLOCK, (b + 1) * BLOCK)
+                    dk_acc[g, part, :] += gr_in[g, j, 0].astype(jnp.float32) * (here * math.sqrt(HEAD_DIM))
+                    dv_acc[g, part, :] += gr_in[g, j, 1].astype(jnp.float32) * here
+
+        dk_out[:, cols] = (dk_acc[g, 0:tok, :] * scale).astype(jnp.bfloat16)
+        dv_out[:, cols] = dv_acc[g, 0:tok, :].astype(jnp.bfloat16)
+
+    p0 = z // 2
+    p1 = 1 - p0
+    quarter = heads // 4
+    softmaxes(0, quarter)
+    own_event(1)
+    xy_event(0)
+    softmaxes(quarter, 2 * quarter)
+    own_event(2)
+    xy_event(1)
+    diag_event(0)
+    softmaxes(2 * quarter, 3 * quarter)
+    own_event(3)
+    xy_event(2)
+    diag_event(1)
+    softmaxes(3 * quarter, 4 * quarter)
+    og_copy.wait()
+    unit(d_own, p0)
+    xy_event(3)
+    diag_event(2)
+    unit(d_x, p0)
+    for i in (0, 1):
+        sib_wait(i, (0, 2))
+    unit(d_sib, p0)
+    diag_event(3)
+    unit(d_own, p1)
+    send_grads(d_own)
+    for i in (0, 1):
+        sib_wait(i, (1, 3))
+    unit(d_xs, p0)
+    for i in (2, 3):
+        sib_wait(i, (0, 2))
+    unit(d_sib, p1)
+    send_grads(d_sib)
+    unit(d_x, p1)
+    send_grads(d_x)
+    for i in (2, 3):
+        sib_wait(i, (1, 3))
+    unit(d_xs, p1)
+    send_grads(d_xs)
+    lo_out[...] = lo_acc[...].astype(jnp.bfloat16)
+    for g in (d_own, d_sib, d_x, d_xs):
+        finish_grads(g)
+
+    def done(c):
+        c.wait_send()
+
+    for i in range(n_z):
+        zz = z_order[i]
+        z_sends(zz, done)
+        x_copy(zz, d_own).wait_send()
+        y_copy(zz, y).wait_send()
+        yh_copy(zz, y).wait_send()
+        xh_copy(zz, d_own).wait_send()
+        for kind in range(4):
+            s_copy(zz, kind, False).wait_send()
+    for j in range(levels):
+        @pl.when(seq + (1 << j) < n_seq)
+        def _():
+            for c in kv_copies(j):
+                c.wait_send()
+
+        @pl.when(seq >= (1 << j))
+        def _():
+            for g in range(kv_heads):
+                gr_copy(g, j, True).wait_send()
+
+
+def fused_shards(queries, key_states, value_states, block_picks, out_weight, out_grad):
+    q, k, v, og = queries[0], key_states[0], value_states[0], out_grad[0]
+    tok, q_cols = q.shape
+    kv_cols = k.shape[1]
+    n_seq = lax.axis_size("seq")
+    levels = n_seq.bit_length() - 1
+    keys = tok + levels * BLOCK
+    heads, kv_heads = q_cols // HEAD_DIM, kv_cols // HEAD_DIM
+    out_width = out_weight.shape[1]
+    n_z = n_seq // 2
+    vmem = pl.BlockSpec(memory_space=pltpu.VMEM)
+    hbm = pl.BlockSpec(memory_space=pl.ANY)
+    smem = pl.BlockSpec(memory_space=pltpu.SMEM)
+    low = jnp.bfloat16
+    dma = pltpu.SemaphoreType.DMA
+    outs = pl.pallas_call(
+        fused_kernel,
+        out_shape=(
+            jax.ShapeDtypeStruct((tok, out_width), low),
+            jax.ShapeDtypeStruct((tok, q_cols), low),
+            jax.ShapeDtypeStruct((tok, kv_cols), low),
+            jax.ShapeDtypeStruct((tok, kv_cols), low),
+        ),
+        in_specs=[smem, hbm, vmem, vmem, vmem, hbm],
+        out_specs=(vmem, vmem, vmem, vmem),
+        scratch_shapes=[
+            pltpu.VMEM((tok, q_cols), low),
+            pltpu.VMEM((tok, out_width), low),
+            pltpu.VMEM((q_cols, out_width), low),
+            pltpu.VMEM((keys, kv_cols), low),
+            pltpu.VMEM((keys, kv_cols), low),
+            pltpu.VMEM((kv_cols, keys), low),
+            pltpu.VMEM((kv_cols, keys), low),
+            pltpu.VMEM((levels, 2, BLOCK, kv_cols), low),
+            pltpu.VMEM((heads, keys, tok), low),
+            pltpu.VMEM((q_cols, tok), low),
+            pltpu.VMEM((tok, out_width), jnp.float32),
+            pltpu.VMEM((kv_heads, keys, HEAD_DIM), jnp.float32),
+            pltpu.VMEM((kv_heads, keys, HEAD_DIM), jnp.float32),
+            pltpu.VMEM((kv_heads, levels, 2, BLOCK, HEAD_DIM), low),
+            pltpu.VMEM((kv_heads, levels, 2, BLOCK, HEAD_DIM), low),
+            dma((2,)),
+            dma((levels, 2)),
+            dma((levels, 2)),
+            dma((2, n_z)),
+            dma((n_z,)),
+            dma((n_z,)),
+            dma((4, n_z)),
+            dma((n_z,)),
+            dma((n_z,)),
+            dma((n_z,)),
+            dma((n_z,)),
+            dma((n_z,)),
+            dma((4, n_z)),
+            dma((n_z,)),
+            dma((n_z,)),
+            dma((kv_heads, levels)),
+            dma((kv_heads, levels)),
+        ],
+        compiler_params=pltpu.CompilerParams(
+            collective_id=0, has_side_effects=True, vmem_limit_bytes=56 * 1024 * 1024
+        ),
+    )(block_picks, q, k, v, out_weight, og)
+    return tuple(out[None] for out in outs)
+
+
 def solution(mesh):
+    fused = mesh.shape["dp"] == 4 and mesh.shape["seq"] == 8
     return jax.shard_map(
-        shards,
+        fused_shards if fused else shards,
         mesh=mesh,
         in_specs=(
             P("dp", "seq", None),

time: 235 us -> 93.8 us (0.40)
  Pallas kernels: 0 us -> 85.2 us
  waiting for transfers between devices: 73.5 us -> 0 us
  matrix products: 59.8 us -> 0 us
  starting transfers between devices: 28.3 us -> 0 us
  local copies, waits for them, and re-layouts: 32.5 us -> 6.49 us
  other arithmetic: 21.5 us -> 0 us
  between operations: 18.4 us -> 0.66 us
    pallas_call x0 -> x1, Pallas kernels: none -> 85.2 us  [fused_shards(): pl.pallas_call(fused_kernel, out_shape=(jax.ShapeDtypeStruct((tok, out_wi...]
    dot_general x22 -> x0, matrix products: 49.8 us -> none  [the longest x4 10.9 us: shards(): jnp.einsum('gts,tgd->sd', probs_low, grad_group, preferred_element_type=j...]
    all_gather x1 -> x0, waiting for transfers between devices: 39.2 us -> none  [shards(): whole_weight = lax.all_gather(out_weight, ('dp', 'seq'), axis=0, tiled=True)]
    ppermute x12 -> x0, waiting for transfers between devices: 33.7 us -> none  [shifted(): return lax.ppermute(block, axis, route)]
    ppermute x12 -> x0, starting transfers between devices: 28.2 us -> none  [shifted(): return lax.ppermute(block, axis, route)]
    unnamed x98 -> x13, local copies, waits for them, and re-layouts: 16.7 us -> 6.49 us
    sub x4 -> x0, matrix products: 9.91 us -> none  [shards(): exp_scores = jnp.exp(scores - row_max)]
    dynamic_slice x10 -> x0, local copies, waits for them, and re-layouts: 7.37 us -> none  [the longest x6 5.03 us: shards(): far_values.append(lax.dynamic_slice_in_dim(got_values, row_begin, BLOCK, 0))]
  transfers between devices with their start and end apart: 13 -> 0, of which waited for: 6 -> 0; matrix products, arithmetic and copies ran while one was open for 21% -> 0% of each run, Pallas kernels for 0% -> 0%
where the time goes in v1:
time: 93.8 us; the launch traced here: 92.3 us
  Pallas kernels  85.2 us (91%)
  local copies, waits for them, and re-layouts  6.49 us (7%)
    pallas_call x1, Pallas kernels, fused_shards(): pl.pallas_call(fused_kernel, out_shape=(jax.ShapeDtypeStruct((tok, out_wi...  85.2 us
    unnamed x13, local copies, waits for them, and re-layouts  6.49 us

profile of v1, /device:TPU:0, one launch (start us, length us, event | category | flops | bytes accessed | tf_op | source)
XLA Modules:
  0.0 92.3 jit_solution(15503075377323488326)
XLA Ops:
  0.6 0.0 copy-start.3
  0.6 0.7 copy-done.3
  1.3 0.6 copy.10.picks
  1.9 85.2 %shard_map.93 = (bf16[256,2048]{1,0:T(8,128)(2,1)}, bf16[256,2048]{1,0:T(8,128)(2,1)}, bf16[256,512]{1,0:T(8,128)(2,1)}, bf16[256,512]{1,0:T(8,128)(2,1)}) custom-call(s32[1,3,8]{2,1,0:T(4,128)} %copy.10.picks, bf16[256,2048]{1,0:T(8,128)(2,1)} %bitcast.8, bf16[256,512]{1,0:T(8,128)(2,1)} %bitcast.12, bf16[256,512]{1,0:T(8,128)(2,1)} %bitcast.13, ...), custom_call_target="tpu_custom_call" | custom-call | tf_op jit(solution)/shard_map/pallas_call | solution.py:495
  87.1 0.0 copy-start
  87.1 2.4 %copy.15 = bf16[1,256,2048]{2,1,0:T(8,128)(2,1)} copy(bf16[1,256,2048]{2,1,0:T(8,128)(2,1)} %bitcast.11) | data formatting | bytes 2097152
  89.5 0.0 copy-done
  89.5 0.0 copy-start.2
  89.5 1.0 %copy.16 = bf16[1,256,2048]{2,1,0:T(8,128)(2,1)} copy(bf16[1,256,2048]{2,1,0:T(8,128)(2,1)S(1)} %bitcast.10) | data formatting | bytes 2097152
  90.4 0.1 copy-done.2
  90.6 0.0 copy-start.1
  90.6 0.7 copy.17
  91.3 0.3 copy-done.1
  91.6 0.7 copy.18
Async XLA Ops:
  0.6 0.7 copy-start.3
  87.1 2.4 %copy-start = (bf16[256,2048]{1,0:T(8,128)(2,1)S(1)}, bf16[256,2048]{1,0:T(8,128)(2,1)}, u32[]{:S(2)}) copy-start(bf16[256,2048]{1,0:T(8,128)(2,1)} %get-tuple-element.9) | copy-start | bytes 3145732
  89.5 1.1 %copy-start.2 = (bf16[256,512]{1,0:T(8,128)(2,1)S(1)}, bf16[256,512]{1,0:T(8,128)(2,1)}, u32[]{:S(2)}) copy-start(bf16[256,512]{1,0:T(8,128)(2,1)} %get-tuple-element.10) | copy-start | bytes 786436
  90.6 1.0 %copy-start.1 = (bf16[256,512]{1,0:T(8,128)(2,1)S(1)}, bf16[256,512]{1,0:T(8,128)(2,1)}, u32[]{:S(2)}) copy-start(bf16[256,512]{1,0:T(8,128)(2,1)} %get-tuple-element.11) | copy-start | bytes 786436

commit v2 on v1

--- a/solution.py
+++ b/solution.py
@@ -151,7 +151,7 @@
 def fused_kernel(
     picks, q_hbm, k_in, v_in, w_in, og_hbm,
     lo_out, dq_out, dk_out, dv_out,
-    q_v, og_v, wbuf, kall, vall, k_t, v_t, kv_stage, probs, attn_t, lo_acc,
+    q_v, og_v, wbuf, kv_all, k_t, v_t, kv_stage, probs, attn_t, lo_acc,
     dk_acc, dv_acc, gr_stage, gr_in,
     in_sem, kv_ssem, kv_rsem, z_ssem, x_ssem, y_ssem, s_ssem, xh_ssem, yh_ssem,
     z_rsem, x_rsem, y_rsem, s_rsem, xh_rsem, yh_rsem, gr_ssem, gr_rsem,
@@ -211,16 +211,20 @@
     def w_half(d, zz, yy, hf):
         return wbuf.at[pl.ds(pl.multiple_of(w_row(d, zz, yy) + hf * half, half), half)]
 
-    for j in range(levels):
-        target = jnp.minimum(seq + (1 << j), n_seq - 1)
-        second = picks[0, j, target].astype(jnp.float32)
-        for i, buf in enumerate((k_in, v_in)):
-            first_rows = buf[0:BLOCK, :].astype(jnp.float32) * (1.0 - second)
-            second_rows = buf[BLOCK : 2 * BLOCK, :].astype(jnp.float32) * second
-            kv_stage[j, i] = (first_rows + second_rows).astype(jnp.bfloat16)
+    def stage_group(g):
+        cols = group_cols(g)
+        for j in range(levels):
+            second = picks[0, j, jnp.minimum(seq + (1 << j), n_seq - 1)].astype(jnp.float32)
+            for i, buf in enumerate((k_in, v_in)):
+                first_rows = buf[0:BLOCK, cols].astype(jnp.float32) * (1.0 - second)
+                second_rows = buf[BLOCK : 2 * BLOCK, cols].astype(jnp.float32) * second
+                kv_stage[g, j, i] = (first_rows + second_rows).astype(jnp.bfloat16)
+
+    def group_cols(g):
+        return pl.ds(pl.multiple_of(g * HEAD_DIM, HEAD_DIM), HEAD_DIM)
+
+    stage_group(d_own)
     wbuf[pl.ds(w_row(dp, z, y), rows), :] = w_in[...]
-    kall[0:tok, :] = k_in[...]
-    vall[0:tok, :] = v_in[...]
     pl.semaphore_wait(barrier, count)
 
     def remote(src, dst, ssem, rsem, dev):
@@ -228,13 +232,16 @@
             src_ref=src, dst_ref=dst, send_sem=ssem, recv_sem=rsem, device_id=dev, device_id_type=MESH
         )
 
-    def kv_copies(j):
-        out = []
-        for i, buf in enumerate((kall, vall)):
-            dst = buf.at[pl.ds(tok + j * BLOCK, BLOCK)]
-            dev = (dp, jnp.minimum(seq + (1 << j), n_seq - 1))
-            out.append(remote(kv_stage.at[j, i], dst, kv_ssem.at[j, i], kv_rsem.at[j, i], dev))
-        return out
+    def kv_copy(g, j):
+        dst = kv_all.at[g, :, pl.ds(tok + j * BLOCK, BLOCK)]
+        dev = (dp, jnp.minimum(seq + (1 << j), n_seq - 1))
+        return remote(kv_stage.at[g, j], dst, kv_ssem.at[g, j], kv_rsem.at[g, j], dev)
+
+    def kv_send(g):
+        for j in range(levels):
+            @pl.when(seq + (1 << j) < n_seq)
+            def _():
+                kv_copy(g, j).start()
 
     z_order = (z, jnp.bitwise_xor(z, 1), jnp.where(z < 2, 2, 1), jnp.where(z < 2, 3, 0))
 
@@ -302,38 +309,30 @@
         for kind in kinds:
             s_copy(z_order[i], kind, True).wait_recv()
 
-    for j in range(levels):
-        @pl.when(seq + (1 << j) < n_seq)
-        def _():
-            for c in kv_copies(j):
-                c.start()
-
+    kv_send(d_own)
     own_event(0)
+    for g in (d_sib, d_x, d_xs):
+        stage_group(g)
 
     for j in range(levels):
         @pl.when(seq < (1 << j))
         def _():
-            for buf in (kall, vall):
-                buf[tok + j * BLOCK : tok + (j + 1) * BLOCK, :] = jnp.zeros((BLOCK, buf.shape[1]), buf.dtype)
-
+            block = slice(tok + j * BLOCK, tok + (j + 1) * BLOCK)
+            kv_all[:, :, block, :] = jnp.zeros((kv_heads, 2, BLOCK, HEAD_DIM), kv_all.dtype)
+
+    for g in range(kv_heads):
+        for i, buf in enumerate((k_in, v_in)):
+            kv_all[g, i, 0:tok, :] = buf[:, g * HEAD_DIM : (g + 1) * HEAD_DIM]
     dk_acc[...] = jnp.zeros_like(dk_acc)
     dv_acc[...] = jnp.zeros_like(dv_acc)
     lo_acc[...] = jnp.zeros_like(lo_acc)
     q_copy.wait()
-    for j in range(levels):
-        @pl.when(seq >= (1 << j))
-        def _():
-            for c in kv_copies(j):
-                c.wait_recv()
-
-    def group_cols(g):
-        return pl.ds(pl.multiple_of(g * HEAD_DIM, HEAD_DIM), HEAD_DIM)
 
     causal = lax.broadcasted_iota(jnp.int32, (tok, tok), 0) <= lax.broadcasted_iota(jnp.int32, (tok, tok), 1)
 
     def softmax_head(h, carry):
         g = h // group_size
-        s = dot(kall[:, group_cols(g)], q_v[:, group_cols(h)], NT)
+        s = dot(kv_all[g, 0], q_v[:, group_cols(h)], NT)
         parts = [jnp.where(causal, s[:tok], neg_fill)]
         for j in range(levels):
             bias = jnp.where(seq >= (1 << j), 0.0, neg_fill).astype(jnp.float32)
@@ -348,15 +347,19 @@
         inv = 1.0 / total
         low = jnp.concatenate([(part * inv).astype(jnp.bfloat16) for part in exps], 0)
         probs[h] = low
-        at = dot(v_t[group_cols(g), :], low, NN)
+        at = dot(v_t[g], low, NN)
         attn_t[pl.ds(pl.multiple_of(h * HEAD_DIM, HEAD_DIM), HEAD_DIM), :] = at.astype(jnp.bfloat16)
         return carry
 
-    k_t[...] = kall[...].T
-    v_t[...] = vall[...].T
-
-    def softmaxes(lo, hi):
-        lax.fori_loop(lo, hi, softmax_head, 0)
+    def softmaxes(g):
+        for j in range(levels):
+            @pl.when(seq >= (1 << j))
+            def _():
+                kv_copy(g, j).wait_recv()
+
+        k_t[g] = kv_all[g, 0].T
+        v_t[g] = kv_all[g, 1].T
+        lax.fori_loop(g * group_size, (g + 1) * group_size, softmax_head, 0)
 
     def unit(g, p):
         base = pl.multiple_of(g * group_rows + p * pair_rows, pair_rows)
@@ -364,7 +367,6 @@
         g_t = dot(wp, og_v[...], NT).astype(jnp.bfloat16)
         a_t = attn_t[pl.ds(base, pair_rows), :]
         lo_acc[...] += dot(a_t, wp, TN)
-        cols = group_cols(g)
         dk = dk_acc[g]
         dv = dv_acc[g]
         for i in range(pair_heads):
@@ -373,9 +375,9 @@
             ah = a_t[i * HEAD_DIM : (i + 1) * HEAD_DIM]
             delta = jnp.sum(gh.astype(jnp.float32) * ah.astype(jnp.float32), axis=0, keepdims=True)
             low = probs[h]
-            dprob = dot(vall[:, cols], gh, NN)
+            dprob = dot(kv_all[g, 1], gh, NN)
             ds = (low.astype(jnp.float32) * (dprob - delta)).astype(jnp.bfloat16)
-            dq_t = dot(k_t[cols, :], ds, NN) * scale
+            dq_t = dot(k_t[g], ds, NN) * scale
             dq_out[:, group_cols(h)] = dq_t.T.astype(jnp.bfloat16)
             dk += dot(ds, q_v[:, group_cols(h)], NN)
             dv += dot(low, gh, NT)
@@ -412,41 +414,41 @@
 
     p0 = z // 2
     p1 = 1 - p0
-    quarter = heads // 4
-    softmaxes(0, quarter)
     own_event(1)
     xy_event(0)
-    softmaxes(quarter, 2 * quarter)
+    kv_send(d_sib)
+    softmaxes(d_own)
     own_event(2)
     xy_event(1)
+    kv_send(d_x)
     diag_event(0)
-    softmaxes(2 * quarter, 3 * quarter)
+    og_copy.wait()
+    unit(d_own, p0)
     own_event(3)
     xy_event(2)
+    kv_send(d_xs)
     diag_event(1)
-    softmaxes(3 * quarter, 4 * quarter)
-    og_copy.wait()
-    unit(d_own, p0)
-    xy_event(3)
-    diag_event(2)
-    unit(d_x, p0)
+    softmaxes(d_sib)
     for i in (0, 1):
         sib_wait(i, (0, 2))
     unit(d_sib, p0)
-    diag_event(3)
+    xy_event(3)
+    diag_event(2)
     unit(d_own, p1)
     send_grads(d_own)
-    for i in (0, 1):
-        sib_wait(i, (1, 3))
-    unit(d_xs, p0)
     for i in (2, 3):
         sib_wait(i, (0, 2))
     unit(d_sib, p1)
     send_grads(d_sib)
+    softmaxes(d_x)
+    unit(d_x, p0)
+    diag_event(3)
+    softmaxes(d_xs)
     unit(d_x, p1)
     send_grads(d_x)
-    for i in (2, 3):
+    for i in range(n_z):
         sib_wait(i, (1, 3))
+    unit(d_xs, p0)
     unit(d_xs, p1)
     send_grads(d_xs)
     lo_out[...] = lo_acc[...].astype(jnp.bfloat16)
@@ -468,8 +470,8 @@
     for j in range(levels):
         @pl.when(seq + (1 << j) < n_seq)
         def _():
-            for c in kv_copies(j):
-                c.wait_send()
+            for g in range(kv_heads):
+                kv_copy(g, j).wait_send()
 
         @pl.when(seq >= (1 << j))
         def _():
@@ -506,11 +508,10 @@
             pltpu.VMEM((tok, q_cols), low),
             pltpu.VMEM((tok, out_width), low),
             pltpu.VMEM((q_cols, out_width), low),
-            pltpu.VMEM((keys, kv_cols), low),
-            pltpu.VMEM((keys, kv_cols), low),
-            pltpu.VMEM((kv_cols, keys), low),
-            pltpu.VMEM((kv_cols, keys), low),
-            pltpu.VMEM((levels, 2, BLOCK, kv_cols), low),
+            pltpu.VMEM((kv_heads, 2, keys, HEAD_DIM), low),
+            pltpu.VMEM((kv_heads, HEAD_DIM, keys), low),
+            pltpu.VMEM((kv_heads, HEAD_DIM, keys), low),
+            pltpu.VMEM((kv_heads, levels, 2, BLOCK, HEAD_DIM), low),
             pltpu.VMEM((heads, keys, tok), low),
             pltpu.VMEM((q_cols, tok), low),
             pltpu.VMEM((tok, out_width), jnp.float32),
@@ -519,8 +520,8 @@
             pltpu.VMEM((kv_heads, levels, 2, BLOCK, HEAD_DIM), low),
             pltpu.VMEM((kv_heads, levels, 2, BLOCK, HEAD_DIM), low),
             dma((2,)),
-            dma((levels, 2)),
-            dma((levels, 2)),
+            dma((kv_heads, levels)),
+            dma((kv_heads, levels)),
             dma((2, n_z)),
             dma((n_z,)),
             dma((n_z,)),

time: 93.8 us -> 81.2 us (0.87); the launches traced: 92.3 us -> 81 us
  Pallas kernels: 85.2 us -> 73.8 us
    pallas_call x1, Pallas kernels: 85.2 us -> 73.8 us  [fused_shards(): pl.pallas_call(fused_kernel, out_shape=(jax.ShapeDtypeStruct((tok, out_wi...]
where the time goes in v2:
time: 81.2 us; the launch traced here: 81 us
  Pallas kernels  73.8 us (91%)
  local copies, waits for them, and re-layouts  6.49 us (8%)
    pallas_call x1, Pallas kernels, fused_shards(): pl.pallas_call(fused_kernel, out_shape=(jax.ShapeDtypeStruct((tok, out_wi...  73.8 us
    unnamed x13, local copies, waits for them, and re-layouts  6.49 us

profile of v2, /device:TPU:0, one launch (start us, length us, event | category | flops | bytes accessed | tf_op | source)
XLA Modules:
  0.0 81.0 jit_solution(5335400807280656302)
XLA Ops:
  0.6 0.0 copy-start.3
  0.6 0.7 copy-done.3
  1.3 0.6 copy.10.picks
  1.9 73.8 %shard_map.93 = (bf16[256,2048]{1,0:T(8,128)(2,1)}, bf16[256,2048]{1,0:T(8,128)(2,1)}, bf16[256,512]{1,0:T(8,128)(2,1)}, bf16[256,512]{1,0:T(8,128)(2,1)}) custom-call(s32[1,3,8]{2,1,0:T(4,128)} %copy.10.picks, bf16[256,2048]{1,0:T(8,128)(2,1)} %bitcast.8, bf16[256,512]{1,0:T(8,128)(2,1)} %bitcast.12, bf16[256,512]{1,0:T(8,128)(2,1)} %bitcast.13, ...), custom_call_target="tpu_custom_call" | custom-call | tf_op jit(solution)/shard_map/pallas_call | solution.py:497
  75.7 0.0 copy-start
  75.7 2.4 %copy.15 = bf16[1,256,2048]{2,1,0:T(8,128)(2,1)} copy(bf16[1,256,2048]{2,1,0:T(8,128)(2,1)} %bitcast.11) | data formatting | bytes 2097152
  78.1 0.0 copy-done
  78.1 0.0 copy-start.2
  78.1 1.0 %copy.16 = bf16[1,256,2048]{2,1,0:T(8,128)(2,1)} copy(bf16[1,256,2048]{2,1,0:T(8,128)(2,1)S(1)} %bitcast.10) | data formatting | bytes 2097152
  79.1 0.1 copy-done.2
  79.2 0.0 copy-start.1
  79.2 0.7 copy.17
  79.9 0.3 copy-done.1
  80.2 0.7 copy.18
Async XLA Ops:
  0.6 0.7 copy-start.3
  75.7 2.4 %copy-start = (bf16[256,2048]{1,0:T(8,128)(2,1)S(1)}, bf16[256,2048]{1,0:T(8,128)(2,1)}, u32[]{:S(2)}) copy-start(bf16[256,2048]{1,0:T(8,128)(2,1)} %get-tuple-element.9) | copy-start | bytes 3145732
  78.1 1.1 %copy-start.2 = (bf16[256,512]{1,0:T(8,128)(2,1)S(1)}, bf16[256,512]{1,0:T(8,128)(2,1)}, u32[]{:S(2)}) copy-start(bf16[256,512]{1,0:T(8,128)(2,1)} %get-tuple-element.10) | copy-start | bytes 786436
  79.2 1.0 %copy-start.1 = (bf16[256,512]{1,0:T(8,128)(2,1)S(1)}, bf16[256,512]{1,0:T(8,128)(2,1)}, u32[]{:S(2)}) copy-start(bf16[256,512]{1,0:T(8,128)(2,1)} %get-tuple-element.11) | copy-start | bytes 786436

commit v3 on v2

--- a/solution.py
+++ b/solution.py
@@ -293,11 +293,13 @@
     def xy_event(i):
         zz = z_order[i]
         x_copy(zz, d_x).wait_recv()
-        yh_copy(zz, y).start()
         s_copy(zz, 1, False).start()
         y_copy(zz, 1 - y).wait_recv()
-        xh_copy(zz, d_own).start()
         s_copy(zz, 2, False).start()
+
+    def half_event(i):
+        yh_copy(z_order[i], y).start()
+        xh_copy(z_order[i], d_own).start()
 
     def diag_event(i):
         zz = z_order[i]
@@ -421,25 +423,29 @@
     own_event(2)
     xy_event(1)
     kv_send(d_x)
-    diag_event(0)
     og_copy.wait()
     unit(d_own, p0)
     own_event(3)
+    half_event(0)
+    half_event(1)
+    kv_send(d_xs)
     xy_event(2)
-    kv_send(d_xs)
-    diag_event(1)
+    half_event(2)
+    xy_event(3)
+    half_event(3)
+    unit(d_own, p1)
+    send_grads(d_own)
     softmaxes(d_sib)
+    diag_event(0)
     for i in (0, 1):
         sib_wait(i, (0, 2))
     unit(d_sib, p0)
-    xy_event(3)
-    diag_event(2)
-    unit(d_own, p1)
-    send_grads(d_own)
+    diag_event(1)
     for i in (2, 3):
         sib_wait(i, (0, 2))
     unit(d_sib, p1)
     send_grads(d_sib)
+    diag_event(2)
     softmaxes(d_x)
     unit(d_x, p0)
     diag_event(3)

time: 81.2 us -> 81.3 us (level)
  the two profiles are of different devices: /device:TPU:0 before, /device:TPU:8 now
where the time goes in v3:
time: 81.3 us; the launch traced here: 81.1 us
  Pallas kernels  73.9 us (91%)
  local copies, waits for them, and re-layouts  6.49 us (8%)
    pallas_call x1, Pallas kernels, fused_shards(): pl.pallas_call(fused_kernel, out_shape=(jax.ShapeDtypeStruct((tok, out_wi...  73.9 us
    unnamed x13, local copies, waits for them, and re-layouts  6.49 us

profile of v3, /device:TPU:8, one launch (start us, length us, event | category | flops | bytes accessed | tf_op | source)
XLA Modules:
  0.0 81.1 jit_solution(7186836357646734740)
XLA Ops:
  0.6 0.0 copy-start.3
  0.6 0.7 copy-done.3
  1.3 0.6 copy.10.picks
  1.9 73.9 %shard_map.93 = (bf16[256,2048]{1,0:T(8,128)(2,1)}, bf16[256,2048]{1,0:T(8,128)(2,1)}, bf16[256,512]{1,0:T(8,128)(2,1)}, bf16[256,512]{1,0:T(8,128)(2,1)}) custom-call(s32[1,3,8]{2,1,0:T(4,128)} %copy.10.picks, bf16[256,2048]{1,0:T(8,128)(2,1)} %bitcast.8, bf16[256,512]{1,0:T(8,128)(2,1)} %bitcast.12, bf16[256,512]{1,0:T(8,128)(2,1)} %bitcast.13, ...), custom_call_target="tpu_custom_call" | custom-call | tf_op jit(solution)/shard_map/pallas_call | solution.py:503
  75.8 0.0 copy-start
  75.8 2.4 %copy.15 = bf16[1,256,2048]{2,1,0:T(8,128)(2,1)} copy(bf16[1,256,2048]{2,1,0:T(8,128)(2,1)} %bitcast.11) | data formatting | bytes 2097152
  78.2 0.0 copy-done
  78.2 0.0 copy-start.2
  78.2 1.0 %copy.16 = bf16[1,256,2048]{2,1,0:T(8,128)(2,1)} copy(bf16[1,256,2048]{2,1,0:T(8,128)(2,1)S(1)} %bitcast.10) | data formatting | bytes 2097152
  79.2 0.1 copy-done.2
  79.3 0.0 copy-start.1
  79.3 0.7 copy.17
  80.0 0.3 copy-done.1
  80.4 0.7 copy.18
Async XLA Ops:
  0.6 0.7 copy-start.3
  75.8 2.4 %copy-start = (bf16[256,2048]{1,0:T(8,128)(2,1)S(1)}, bf16[256,2048]{1,0:T(8,128)(2,1)}, u32[]{:S(2)}) copy-start(bf16[256,2048]{1,0:T(8,128)(2,1)} %get-tuple-element.9) | copy-start | bytes 3145732
  78.2 1.1 %copy-start.2 = (bf16[256,512]{1,0:T(8,128)(2,1)S(1)}, bf16[256,512]{1,0:T(8,128)(2,1)}, u32[]{:S(2)}) copy-start(bf16[256,512]{1,0:T(8,128)(2,1)} %get-tuple-element.10) | copy-start | bytes 786436
  79.3 1.0 %copy-start.1 = (bf16[256,512]{1,0:T(8,128)(2,1)S(1)}, bf16[256,512]{1,0:T(8,128)(2,1)}, u32[]{:S(2)}) copy-start(bf16[256,512]{1,0:T(8,128)(2,1)} %get-tuple-element.11) | copy-start | bytes 786436
